TPU v7x, 32 devices: a whole 2x2x4 slice. The times are simulated.
32 devices in a mesh: row: 4 (over z), col: 8 (over y, x, core).
Axes of the slice: x: 2, y: 2, z: 4, core: 2. Of those that a mesh axis runs over, the one named last changes fastest.
Arguments:
- activations: bfloat16 [96, 48, 3072], P('row', None, 'col'), may hold values from -30 to 30
- cotangent: bfloat16 [96, 48, 3072], P('row', None, 'col'), may hold values from -6 to 6
- kernel: float32 [7, 7, 3072], P(None, None, 'col'), may hold values from -0.875 to 0.875
- ln_gain: float32 [3072], replicated, may hold values from 0.25 to 1.75
- ln_bias: float32 [3072], replicated, may hold values from -3 to 3
- w_expand: bfloat16 [3072, 12288], P('row', 'col'), may hold values from -0.5 to 0.5
- b_expand: float32 [12288], P('col'), may hold values from -3 to 3
- w_reduce: bfloat16 [12288, 3072], P('col', 'row'), may hold values from -0.078125 to 0.078125
- b_reduce: float32 [3072], P('col'), may hold values from -3 to 3
- layer_scale: float32 [3072], P('col'), may hold values from 0.3 to 1.5
Outputs:
- block_out: bfloat16 [96, 48, 3072], P('row', None, 'col')
- grad_input: bfloat16 [96, 48, 3072], P('row', None, 'col')
All inputs are finite; a program needn't handle non-finite values.
Results may differ from a plain program's by a relative error of at most 0.015.
Values may be sent and summed in bfloat16 or wider, within the bound.
A program may use at most 128 MiB of HBM per device.

v0:
```python
import jax
import jax.numpy as jnp
from jax import lax
from jax.sharding import PartitionSpec as P

H = 48
epsilon = 1e-06
root_half = 0.7071067811865476
density_scale = 0.3989422804014327


def spatial_mix(padded, weights, height):
    row_count = padded.shape[0] - 6
    col_count = padded.shape[1] - 6
    out_rows = jnp.arange(row_count, dtype=jnp.int32)
    running = jnp.zeros((row_count, col_count, padded.shape[2]), jnp.float32)
    for row_off in range(7):
        source = out_rows + (row_off - 3)
        inside = source // height == out_rows // height
        band = jnp.zeros_like(running)
        for col_off in range(7):
            band = (
                band
                + weights[row_off, col_off]
                * padded[row_off : row_off + row_count, col_off : col_off + col_count]
            )
        running = running + jnp.where(inside[:, None, None], band, jnp.zeros_like(band))
    return running


def gelu_slope(preact):
    cumulative = 0.5 * (1.0 + jax.scipy.special.erf(preact * root_half))
    return cumulative + preact * jnp.exp(-0.5 * preact * preact) * density_scale


def channel_sums(first_sum, second_sum):
    return lax.psum((first_sum, second_sum), "col")


def body(
    activations,
    cotangent,
    kernel,
    ln_gain,
    ln_bias,
    w_expand,
    b_expand,
    w_reduce,
    b_reduce,
    layer_scale,
):
    row_count, grid_width, narrow = activations.shape
    channels = narrow * lax.axis_size("col")
    col_start = lax.axis_index("col") * narrow
    tokens = row_count * grid_width
    flipped = kernel[::-1, ::-1]

    def mixing(source_field, weights):
        gathered = lax.all_to_all(source_field, "row", split_axis=2, concat_axis=0, tiled=True)
        per_device = gathered.shape[2]
        subset = lax.dynamic_slice_in_dim(
            weights, lax.axis_index("row") * per_device, per_device, 2
        )
        padded = jnp.pad(gathered, ((3, 3), (3, 3), (0, 0))).astype(jnp.float32)
        mixed_out = spatial_mix(padded, subset, H).astype(jnp.bfloat16)
        return lax.all_to_all(mixed_out, "row", split_axis=0, concat_axis=2, tiled=True)

    mixed_bf = mixing(activations, kernel)
    mixed_flat = lax.optimization_barrier(mixed_bf).reshape(tokens, narrow)
    expand_full, reduce_full = (
        lax.all_gather(w_expand, "row", axis=0, tiled=True),
        lax.all_gather(w_reduce, "row", axis=1, tiled=True),
    )
    local_mixed = mixed_flat.astype(jnp.float32)
    row_sum, square_sum = channel_sums(
        jnp.sum(local_mixed, 1), jnp.sum(local_mixed * local_mixed, 1)
    )
    row_mean = row_sum[:, None] / channels
    square = square_sum[:, None] / channels
    inv_std = lax.rsqrt(square - row_mean * row_mean + epsilon)
    normal_local = (local_mixed - row_mean) * inv_std
    local_gain = lax.dynamic_slice_in_dim(ln_gain, col_start, narrow)
    local_shift = lax.dynamic_slice_in_dim(ln_bias, col_start, narrow)
    normed = (normal_local * local_gain + local_shift).astype(jnp.bfloat16)
    panel = expand_full
    preact = jnp.dot(
        lax.all_gather(normed, "col", axis=1, tiled=True), panel, preferred_element_type=jnp.float32
    )
    preact = preact + b_expand
    hidden = jax.nn.gelu(preact, approximate=False).astype(jnp.bfloat16)
    panel = reduce_full
    branch_turned = lax.psum_scatter(
        lax.dot_general(
            panel, hidden, (((0,), (1,)), ((), ())), preferred_element_type=jnp.float32
        ).astype(jnp.bfloat16),
        "col",
        scatter_dimension=0,
        tiled=True,
    ).astype(jnp.float32)
    branch_out = branch_turned.T + b_reduce
    act_f = activations.astype(jnp.float32)
    block_out = (act_f + layer_scale * branch_out.reshape(row_count, grid_width, narrow)).astype(
        jnp.bfloat16
    )
    cot_f = cotangent.astype(jnp.float32)
    grad_branch = (layer_scale * cot_f).reshape(tokens, narrow).astype(jnp.bfloat16)
    panel = reduce_full
    grad_hidden = lax.dot_general(
        lax.all_gather(grad_branch, "col", axis=1, tiled=True),
        panel,
        (((1,), (1,)), ((), ())),
        preferred_element_type=jnp.float32,
    )
    grad_preact = (grad_hidden * gelu_slope(preact)).astype(jnp.bfloat16)
    panel = expand_full
    grad_turned = lax.psum_scatter(
        lax.dot_general(
            panel, grad_preact, (((1,), (1,)), ((), ())), preferred_element_type=jnp.float32
        ).astype(jnp.bfloat16),
        "col",
        scatter_dimension=0,
        tiled=True,
    ).astype(jnp.float32)
    grad_gain = grad_turned.T * local_gain
    grad_total, grad_cross = channel_sums(
        jnp.sum(grad_gain, 1), jnp.sum(grad_gain * normal_local, 1)
    )
    grad_mixed = inv_std * (
        grad_gain - grad_total[:, None] / channels - normal_local * grad_cross[:, None] / channels
    )
    grad_mixed = grad_mixed.astype(jnp.bfloat16).reshape(row_count, grid_width, narrow)
    grad_spatial = mixing(grad_mixed, flipped)
    grad_input = (cot_f + lax.optimization_barrier(grad_spatial).astype(jnp.float32)).astype(
        jnp.bfloat16
    )
    return (block_out, grad_input)


def solution(mesh):
    return jax.shard_map(
        body,
        mesh=mesh,
        in_specs=(
            P("row", None, "col"),
            P("row", None, "col"),
            P(None, None, "col"),
            P(),
            P(),
            P("row", "col"),
            P("col"),
            P("col", "row"),
            P("col"),
            P("col"),
        ),
        out_specs=(P("row", None, "col"), P("row", None, "col")),
        check_vma=False,
    )
```

profile of v0, /device:TPU:2, one launch (start us, length us, event | category | flops | bytes accessed | tf_op | source)
XLA Modules:
  0.0 833.0 jit_solution(8400221531538594373)
XLA Ops:
  9.8 4.6 reshape.134
  14.4 4.9 all-to-all-start
  23.2 46.9 %all-to-all-done = bf16[4,2,55296]{2,1,0:T(2,128)(2,1)S(1)} async-done(((bf16[4,2,55296]{2,1,0:T(2,128)(2,1)}), bf16[4,2,55296]{2,1,0:T(2,128)(2,1)S(1)}, u32[]{:S(2)}, u32[]{:S(2)}) %all-to-all-start) | async-done | bytes 884768 | tf_op jit(solution)/shard_map/all_to_all | solution.py:59
  76.0 20.2 %fusion.115 = bf16[96,48,96]{2,1,0:T(8,128)(2,1)} fusion(f32[102,54,96]{2,1,0:T(8,128)S(1)} %pad_convert_fusion.1, f32[96]{0:T(128)} %get-tuple-element.105, f32[96]{0:T(128)S(1)} %get-tuple-element.58, f32[96]{0:T(128)S(1)} %get-tuple-element.59, f32[96]{0:T(128)S(1)} %get-tuple-element.60, f32[96]{0:T(128)S(1)} %copy-done.55, f32[96]{0:T(128)S(1)} %copy-done.56, ...), kind=kLoop, calls=%fused_computation.178 | loop fusion | flops 46006272 | bytes 87608256 | tf_op jit(solution)/shard_map/convert_element_type | solution.py:65
  101.3 54.6 %all-to-all-done.1 = bf16[96,48,96]{2,1,0:T(8,128)(2,1)S(1)} async-done(((bf16[96,48,96]{2,1,0:T(8,128)(2,1)}), bf16[96,48,96]{2,1,0:T(8,128)(2,1)S(1)}, u32[]{:S(2)}, u32[]{:S(2)}) %all-to-all-start.1) | async-done | bytes 884768 | tf_op jit(solution)/shard_map/all_to_all | solution.py:66
  158.1 21.4 %all-reduce.3 = (f32[1152]{0:T(1024)S(1)}, f32[1152]{0:T(1024)S(1)}) all-reduce(f32[1152]{0:T(1024)S(1)} %reduce_sum.43, f32[1152]{0:T(1024)S(1)} %reduce_sum.41), channel_id=1, replica_groups=mesh['row'=4,'col'=8] {'col'}, use_global_device_ids=true, to_apply=%region_3.4 | all-reduce | flops 2304 | bytes 18432 | tf_op jit(solution)/shard_map/psum | solution.py:37
  182.8 36.2 %all-gather.7.cloned.1.call-done = bf16[3072,1536]{1,0:T(8,128)(2,1)} async-done(((bf16[768,1536]{1,0:T(8,128)(2,1)}), bf16[3072,1536]{1,0:T(8,128)(2,1)}) %all-gather.7.cloned.1.call-update) | async-done | bytes 9437200 | tf_op jit(solution)/shard_map/all_gather | solution.py:71
  219.0 51.8 %all-gather.5.cloned.1.call-done = bf16[1152,3072]{1,0:T(8,128)(2,1)} async-done(((bf16[1152,384]{1,0:T(8,128)(2,1)}), bf16[1152,3072]{1,0:T(8,128)(2,1)}) %all-gather.5.cloned.1.call-update) | async-done | bytes 7077904 | tf_op jit(solution)/shard_map/all_gather | solution.py:87
  270.8 17.0 %convolution_add_fusion = f32[1152,1536]{1,0:T(8,128)} fusion(bf16[1152,3072]{1,0:T(8,128)(2,1)} %all-gather.5.cloned.1.call-done, bf16[3072,1536]{1,0:T(8,128)(2,1)} %all-gather.7.cloned.1.call-done, f32[1536]{0:T(1024)S(1)} %copy-done.95), kind=kOutput, calls=%fused_computation.7 | convolution fusion | flops 10873405440 | bytes 23599104 | tf_op jit(solution)/shard_map/dot_general | solution.py:86
  287.8 151.4 %all-gather.9.cloned.1.call-done = bf16[1536,3072]{1,0:T(8,128)(2,1)} async-done(((bf16[1536,768]{1,0:T(8,128)(2,1)}), bf16[1536,3072]{1,0:T(8,128)(2,1)}) %all-gather.9.cloned.1.call-update) | async-done | bytes 9437200 | tf_op jit(solution)/shard_map/all_gather | solution.py:72
  439.2 31.1 %fusion = bf16[3072,1152]{0,1:T(8,128)(2,1)} fusion(bf16[1536,3072]{1,0:T(8,128)(2,1)} %all-gather.9.cloned.1.call-done, f32[1152,1536]{1,0:T(8,128)} %convolution_add_fusion), kind=kOutput, calls=%fused_computation.5 | convolution fusion | flops 10990190592 | bytes 23592960 | tf_op jit(solution)/shard_map/dot_general | solution.py:93
  470.2 9.8 %copy.26 = bf16[3072,1152]{1,0:T(8,128)(2,1)} copy(bf16[3072,1152]{0,1:T(8,128)(2,1)} %fusion) | data formatting | bytes 14155776
  480.2 63.7 %reduce-scatter.7.cloned.1.call-done = bf16[384,1152]{1,0:T(8,128)(2,1)} async-done(((bf16[3072,1152]{1,0:T(8,128)(2,1)}), bf16[384,1152]{1,0:T(8,128)(2,1)}) %reduce-scatter.7.cloned.1.call-update) | async-done | bytes 884752
  547.7 50.2 %all-gather.11.cloned.1.call-done = bf16[1152,3072]{1,0:T(8,128)(2,1)} async-done(((bf16[1152,384]{1,0:T(8,128)(2,1)}), bf16[1152,3072]{1,0:T(8,128)(2,1)}) %all-gather.11.cloned.1.call-update) | async-done | bytes 7077904 | tf_op jit(solution)/shard_map/all_gather | solution.py:109
  597.9 18.7 %fusion.2.clone.4 = bf16[1152,1536]{1,0:T(8,128)(2,1)S(1)} fusion(bf16[1152,3072]{1,0:T(8,128)(2,1)} %all-gather.11.cloned.1.call-done, bf16[1536,3072]{1,0:T(8,128)(2,1)} %all-gather.9.cloned.1.call-done, f32[1152,1536]{1,0:T(8,128)} %convolution_add_fusion), kind=kOutput, calls=%fused_computation.8.clone.clone.clone.1 | convolution fusion | flops 10889330688 | bytes 27131904 | tf_op jit(solution)/shard_map/dot_general | solution.py:108
  616.5 15.6 %fusion.1 = bf16[3072,1152]{0,1:T(8,128)(2,1)} fusion(bf16[3072,1536]{1,0:T(8,128)(2,1)} %all-gather.7.cloned.1.call-done, bf16[1152,1536]{1,0:T(8,128)(2,1)S(1)} %fusion.2.clone.4), kind=kOutput, calls=%fused_computation.6 | convolution fusion | flops 10875174912 | bytes 20054016 | tf_op jit(solution)/shard_map/dot_general | solution.py:117
  632.1 10.3 %copy.28 = bf16[3072,1152]{1,0:T(8,128)(2,1)} copy(bf16[3072,1152]{0,1:T(8,128)(2,1)} %fusion.1) | data formatting | bytes 14155776
  642.5 65.6 %reduce-scatter.9.cloned.1.call-done = bf16[384,1152]{1,0:T(8,128)(2,1)} async-done(((bf16[3072,1152]{1,0:T(8,128)(2,1)}), bf16[384,1152]{1,0:T(8,128)(2,1)}) %reduce-scatter.9.cloned.1.call-update) | async-done | bytes 884752
  710.9 21.2 %all-reduce.2 = (f32[1152]{0:T(1024)S(1)}, f32[1152]{0:T(1024)S(1)}) all-reduce(f32[1152]{0:T(1024)S(1)} %fusion.172, f32[1152]{0:T(1024)S(1)} %fusion.174), channel_id=1, replica_groups=mesh['row'=4,'col'=8] {'col'}, use_global_device_ids=true, to_apply=%region_9.10 | all-reduce | flops 2304 | bytes 18432 | tf_op jit(solution)/shard_map/psum | solution.py:37
  734.4 4.6 reshape.136
  739.1 4.6 all-to-all-start.2
  744.8 22.0 %all-to-all-done.2 = bf16[4,2,55296]{2,1,0:T(2,128)(2,1)S(1)} async-done(((bf16[4,2,55296]{2,1,0:T(2,128)(2,1)}), bf16[4,2,55296]{2,1,0:T(2,128)(2,1)S(1)}, u32[]{:S(2)}, u32[]{:S(2)}) %all-to-all-start.2) | async-done | bytes 884768 | tf_op jit(solution)/shard_map/all_to_all | solution.py:59
  772.6 19.4 %fusion.60 = bf16[96,48,96]{2,1,0:T(8,128)(2,1)S(1)} fusion(f32[102,54,96]{2,1,0:T(8,128)S(1)} %pad_convert_fusion, f32[96]{0:T(128)} %get-tuple-element.56, f32[96]{0:T(128)S(1)} %get-tuple-element.9, f32[96]{0:T(128)S(1)} %get-tuple-element.10, f32[96]{0:T(128)S(1)} %get-tuple-element.11, f32[96]{0:T(128)S(1)} %copy-done.15, f32[96]{0:T(128)S(1)} %copy-done.16, ...), kind=kLoop, calls=%fused_computation.74 | loop fusion | flops 46006272 | bytes 87608256 | tf_op jit(solution)/shard_map/convert_element_type | solution.py:65
  792.1 31.0 %all_to_all.72 = bf16[96,48,96]{2,1,0:T(8,128)(2,1)S(1)} all-to-all(bf16[96,48,96]{2,1,0:T(8,128)(2,1)S(1)} %fusion.60), channel_id=1, replica_groups=mesh['row'=4,'col'=8] {'row'}, dimensions={0} | all-to-all | bytes 1769472 | tf_op jit(solution)/shard_map/all_to_all | solution.py:66
  (241 shorter events, 40.5 us)
Async XLA Ops:
  7.2 1.2 copy-start.2
  7.2 211.9 %all-gather.7.cloned.1.call-start = ((), (), s32[]{:S(2)}) async-start(), calls=%async_computation.7 | async-start | bytes 11796480 | tf_op jit(solution)/shard_map/all_gather | solution.py:71
  14.4 55.7 %all-to-all-start = ((bf16[4,2,55296]{2,1,0:T(2,128)(2,1)}), bf16[4,2,55296]{2,1,0:T(2,128)(2,1)S(1)}, u32[]{:S(2)}, u32[]{:S(2)}) async-start(bf16[4,2,55296]{2,1,0:T(2,128)(2,1)} %reshape.134), calls=%async_computation | async-start | bytes 1769472 | tf_op jit(solution)/shard_map/all_to_all | solution.py:59
  74.8 0.8 copy-start.55
  96.2 59.7 %all-to-all-start.1 = ((bf16[96,48,96]{2,1,0:T(8,128)(2,1)}), bf16[96,48,96]{2,1,0:T(8,128)(2,1)S(1)}, u32[]{:S(2)}, u32[]{:S(2)}) async-start(bf16[96,48,96]{2,1,0:T(8,128)(2,1)} %fusion.115), calls=%async_computation.1 | async-start | bytes 2359296 | tf_op jit(solution)/shard_map/all_to_all | solution.py:66
  99.7 171.1 %all-gather.5.cloned.1.call-start = ((), (), s32[]{:S(2)}) async-start(), calls=%async_computation.6 | async-start | bytes 7962624 | tf_op jit(solution)/shard_map/all_gather | solution.py:87
  100.5 79.1 %copy-start.11 = (f32[384]{0:T(512)}, f32[384]{0:T(512)S(1)}, u32[]{:S(2)}) copy-start(f32[384]{0:T(512)S(1)} %dynamic_slice.13) | copy-start | bytes 4612
  157.5 24.7 %copy-start = (bf16[24,48,384]{2,1,0:T(8,128)(2,1)}, bf16[24,48,384]{2,1,0:T(8,128)(2,1)S(1)}, u32[]{:S(2)}) copy-start(bf16[24,48,384]{2,1,0:T(8,128)(2,1)S(1)} %all_to_all.59) | copy-start | bytes 2654212
  180.2 90.6 %copy-start.95 = (f32[1536]{0:T(1024)S(1)}, f32[1536]{0:T(1024)}, u32[]{:S(2)}) copy-start(f32[1536]{0:T(1024)} %param.16) | copy-start | bytes 18436
  181.5 257.6 %all-gather.9.cloned.1.call-start = ((), (), s32[]{:S(2)}) async-start(), calls=%async_computation.8 | async-start | bytes 11796480 | tf_op jit(solution)/shard_map/all_gather | solution.py:72
  182.3 361.6 %reduce-scatter.7.cloned.1.call-start = ((), (), s32[]{:S(2)}) async-start(), calls=%async_computation.10 | async-start | bytes 7962624
  480.1 65.5 %copy-start.14 = (f32[384]{0:T(512)S(1)}, f32[384]{0:T(512)}, u32[]{:S(2)}) copy-start(f32[384]{0:T(512)} %param.18) | copy-start | bytes 4612
  480.1 65.7 %copy-start.3 = (bf16[24,48,384]{2,1,0:T(8,128)(2,1)S(1)}, bf16[24,48,384]{2,1,0:T(8,128)(2,1)}, u32[]{:S(2)}) copy-start(bf16[24,48,384]{2,1,0:T(8,128)(2,1)} %param.10) | copy-start | bytes 2654212
  480.1 65.7 %copy-start.4 = (bf16[24,48,384]{2,1,0:T(8,128)(2,1)S(1)}, bf16[24,48,384]{2,1,0:T(8,128)(2,1)}, u32[]{:S(2)}) copy-start(bf16[24,48,384]{2,1,0:T(8,128)(2,1)} %param.11) | copy-start | bytes 2654212
  480.1 65.7 %copy-start.13 = (f32[384]{0:T(512)S(1)}, f32[384]{0:T(512)}, u32[]{:S(2)}) copy-start(f32[384]{0:T(512)} %param.19) | copy-start | bytes 4612
  480.1 117.7 %all-gather.11.cloned.1.call-start = ((), (), s32[]{:S(2)}) async-start(), calls=%async_computation.9 | async-start | bytes 7962624 | tf_op jit(solution)/shard_map/all_gather | solution.py:109
  547.5 160.6 %reduce-scatter.9.cloned.1.call-start = ((), (), s32[]{:S(2)}) async-start(), calls=%async_computation.11 | async-start | bytes 7962624
  642.5 67.4 %copy-start.12 = (f32[384]{0:T(512)S(1)}, f32[384]{0:T(512)}, u32[]{:S(2)}) copy-start(f32[384]{0:T(512)} %copy-done.11) | copy-start | bytes 4612
  642.5 67.6 %copy-start.1 = (bf16[24,48,384]{2,1,0:T(8,128)(2,1)S(1)}, bf16[24,48,384]{2,1,0:T(8,128)(2,1)}, u32[]{:S(2)}) copy-start(bf16[24,48,384]{2,1,0:T(8,128)(2,1)} %copy-done) | copy-start | bytes 2654212
  642.5 67.6 %copy-start.8 = (f32[1152]{0:T(1024)S(1)}, f32[1152]{0:T(1024)}, u32[]{:S(2)}) copy-start(f32[1152]{0:T(1024)} %copy-done.7) | copy-start | bytes 13828
  642.5 67.6 %copy-start.10 = (f32[1152]{0:T(1024)S(1)}, f32[1152]{0:T(1024)}, u32[]{:S(2)}) copy-start(f32[1152]{0:T(1024)} %copy-done.9) | copy-start | bytes 13828
  734.4 9.2 %copy-start.6 = (f32[7,7,384]{2,1,0:T(8,128)S(1)}, f32[7,7,384]{2,1,0:T(8,128)}, u32[]{:S(2)}) copy-start(f32[7,7,384]{2,1,0:T(8,128)} %param.12) | copy-start | bytes 225796
  739.1 27.7 %all-to-all-start.2 = ((bf16[4,2,55296]{2,1,0:T(2,128)(2,1)}), bf16[4,2,55296]{2,1,0:T(2,128)(2,1)S(1)}, u32[]{:S(2)}, u32[]{:S(2)}) async-start(bf16[4,2,55296]{2,1,0:T(2,128)(2,1)} %reshape.136), calls=%async_computation.2 | async-start | bytes 1769472 | tf_op jit(solution)/shard_map/all_to_all | solution.py:59
  823.1 1.7 copy-start.5
  (81 other events, 64.5 us)
Sparse Core Ops, SparseCore 0:
  9.6 209.4 all-gather.6
  221.5 49.2 all-gather.4
  272.4 166.7 all-gather.8
  480.2 63.5 reduce-scatter.6
  547.6 50.2 all-gather.10
  642.6 65.4 reduce-scatter.8
where the time goes:
time: 841 us; the launch traced here: 833 us
  waiting for transfers between devices  544 us (65%)
  matrix products  82.3 us (10%)
  blocking collectives  73.6 us (9%)
  local copies, waits for them, and re-layouts  54.9 us (7%)
  other arithmetic  48.8 us (6%)
  between operations  16 us (2%)
  starting transfers between devices  13.9 us (2%)
    all_gather x1, waiting for transfers between devices, body(): lax.all_gather(w_reduce, 'row', axis=1, tiled=True)  151 us
    unnamed x8, waiting for transfers between devices  131 us
    all_to_all x2, waiting for transfers between devices, mixing(): lax.all_to_all(source_field, 'row', split_axis=2, concat_axis=0, tiled=True)  68.8 us
    all_to_all x1, waiting for transfers between devices, mixing(): lax.all_to_all(mixed_out, 'row', split_axis=0, concat_axis=2, tiled=True)  54.6 us
    all_gather x1, waiting for transfers between devices, body(): lax.all_gather(normed, 'col', axis=1, tiled=True)  51.8 us
    all_gather x1, waiting for transfers between devices, body(): lax.all_gather(grad_branch, 'col', axis=1, tiled=True)  50.2 us
    psum x2, blocking collectives, channel_sums(): return lax.psum((first_sum, second_sum), 'col')  42.6 us
    unnamed x201, local copies, waits for them, and re-layouts  40.5 us
  transfers between devices with their start and end apart: 9, of which 9 were waited for; matrix products, arithmetic and copies ran while one was open for 7% of the time, Pallas kernels for 0%

commit v1 on v0

--- a/solution.py
+++ b/solution.py
@@ -7,6 +7,24 @@
 epsilon = 1e-06
 root_half = 0.7071067811865476
 density_scale = 0.3989422804014327
+
+
+def collect(value, axis, dim):
+    ways, here, step = (lax.axis_size(axis), lax.axis_index(axis), value.shape[dim])
+    shape = [n * ways if d == dim else n for d, n in enumerate(value.shape)]
+    full = lax.dynamic_update_slice_in_dim(
+        jnp.zeros(shape, value.dtype), value, here * step, axis=dim
+    )
+    going_up = going_down = value
+    for far in range(1, ways // 2 + 1):
+        going_up = lax.ppermute(going_up, axis, [(d, (d + 1) % ways) for d in range(ways)])
+        full = lax.dynamic_update_slice_in_dim(full, going_up, (here - far) % ways * step, axis=dim)
+        if 2 * far < ways:
+            going_down = lax.ppermute(going_down, axis, [(d, (d - 1) % ways) for d in range(ways)])
+            full = lax.dynamic_update_slice_in_dim(
+                full, going_down, (here + far) % ways * step, axis=dim
+            )
+    return full
 
 
 def spatial_mix(padded, weights, height):
@@ -106,7 +124,7 @@
     grad_branch = (layer_scale * cot_f).reshape(tokens, narrow).astype(jnp.bfloat16)
     panel = reduce_full
     grad_hidden = lax.dot_general(
-        lax.all_gather(grad_branch, "col", axis=1, tiled=True),
+        collect(grad_branch, "col", 1),
         panel,
         (((1,), (1,)), ((), ())),
         preferred_element_type=jnp.float32,

time: 841 us -> 868 us (1.032)
  starting transfers between devices: 13.9 us -> 36.6 us
    all_gather x1 -> x0, waiting for transfers between devices: 50.2 us -> none  [body(): lax.all_gather(grad_branch, 'col', axis=1, tiled=True)]
    ppermute x0 -> x7, waiting for transfers between devices: none -> 43 us  [the longest x4 42.3 us: collect(): lax.ppermute(going_up, axis, [(d, (d + 1) % ways) for d in range(ways)])]
    ppermute x0 -> x7, starting transfers between devices: none -> 22.9 us  [the longest x4 19.1 us: collect(): lax.ppermute(going_up, axis, [(d, (d + 1) % ways) for d in range(ways)])]
    unnamed x8 -> x7, waiting for transfers between devices: 131 us -> 141 us
    unnamed x201 -> x205, local copies, waits for them, and re-layouts: 40.5 us -> 41 us
  transfers between devices with their start and end apart: 9 -> 15, of which waited for: 9 -> 13; matrix products, arithmetic and copies ran while one was open for 7% -> 7% of each run, Pallas kernels for 0% -> 0%
where the time goes in v1:
time: 868 us; the launch traced here: 861 us
  waiting for transfers between devices  546 us (63%)
  matrix products  80.2 us (9%)
  blocking collectives  73.6 us (8%)
  local copies, waits for them, and re-layouts  59.5 us (7%)
  other arithmetic  48.5 us (6%)
  starting transfers between devices  36.6 us (4%)
  between operations  15.7 us (2%)
    all_gather x1, waiting for transfers between devices, body(): lax.all_gather(w_reduce, 'row', axis=1, tiled=True)  151 us
    unnamed x7, waiting for transfers between devices  141 us
    all_to_all x2, waiting for transfers between devices, mixing(): lax.all_to_all(source_field, 'row', split_axis=2, concat_axis=0, tiled=True)  68.8 us
    all_to_all x1, waiting for transfers between devices, mixing(): lax.all_to_all(mixed_out, 'row', split_axis=0, concat_axis=2, tiled=True)  54.6 us
    all_gather x1, waiting for transfers between devices, body(): lax.all_gather(normed, 'col', axis=1, tiled=True)  51.8 us
    psum x2, blocking collectives, channel_sums(): return lax.psum((first_sum, second_sum), 'col')  42.6 us
    ppermute x4, waiting for transfers between devices, collect(): lax.ppermute(going_up, axis, [(d, (d + 1) % ways) for d in range(ways)])  42.3 us
    unnamed x205, local copies, waits for them, and re-layouts  41 us
  transfers between devices with their start and end apart: 15, of which 13 were waited for; matrix products, arithmetic and copies ran while one was open for 7% of the time, Pallas kernels for 0%

profile of v1, /device:TPU:2, one launch (start us, length us, event | category | flops | bytes accessed | tf_op | source)
XLA Modules:
  0.0 860.5 jit_solution(9503604934700878326)
XLA Ops:
  14.4 4.9 all-to-all-start
  23.2 46.8 %all-to-all-done = bf16[4,2,55296]{2,1,0:T(2,128)(2,1)S(1)} async-done(((bf16[4,2,55296]{2,1,0:T(2,128)(2,1)}), bf16[4,2,55296]{2,1,0:T(2,128)(2,1)S(1)}, u32[]{:S(2)}, u32[]{:S(2)}) %all-to-all-start) | async-done | bytes 884768 | tf_op jit(solution)/shard_map/all_to_all | solution.py:77
  76.0 20.1 %fusion.115 = bf16[96,48,96]{2,1,0:T(8,128)(2,1)} fusion(f32[102,54,96]{2,1,0:T(8,128)S(1)} %pad_convert_fusion.1, f32[96]{0:T(128)} %get-tuple-element.105, f32[96]{0:T(128)S(1)} %get-tuple-element.58, f32[96]{0:T(128)S(1)} %get-tuple-element.59, f32[96]{0:T(128)S(1)} %get-tuple-element.60, f32[96]{0:T(128)S(1)} %copy-done.57, f32[96]{0:T(128)S(1)} %copy-done.58, ...), kind=kLoop, calls=%fused_computation.178 | loop fusion | flops 46006272 | bytes 87608256 | tf_op jit(solution)/shard_map/convert_element_type | solution.py:83
  101.2 54.6 %all-to-all-done.1 = bf16[96,48,96]{2,1,0:T(8,128)(2,1)S(1)} async-done(((bf16[96,48,96]{2,1,0:T(8,128)(2,1)}), bf16[96,48,96]{2,1,0:T(8,128)(2,1)S(1)}, u32[]{:S(2)}, u32[]{:S(2)}) %all-to-all-start.1) | async-done | bytes 884768 | tf_op jit(solution)/shard_map/all_to_all | solution.py:84
  158.1 21.4 %all-reduce.3 = (f32[1152]{0:T(1024)S(1)}, f32[1152]{0:T(1024)S(1)}) all-reduce(f32[1152]{0:T(1024)S(1)} %reduce_sum.43, f32[1152]{0:T(1024)S(1)} %reduce_sum.41), channel_id=1, replica_groups=mesh['row'=4,'col'=8] {'col'}, use_global_device_ids=true, to_apply=%region_3.4 | all-reduce | flops 2304 | bytes 18432 | tf_op jit(solution)/shard_map/psum | solution.py:55
  182.8 36.2 %all-gather.6.cloned.1.call-done = bf16[3072,1536]{1,0:T(8,128)(2,1)} async-done(((bf16[768,1536]{1,0:T(8,128)(2,1)}), bf16[3072,1536]{1,0:T(8,128)(2,1)}) %all-gather.6.cloned.1.call-update) | async-done | bytes 9437200 | tf_op jit(solution)/shard_map/all_gather | solution.py:89
  219.0 51.8 %all-gather.4.cloned.1.call-done = bf16[1152,3072]{1,0:T(8,128)(2,1)} async-done(((bf16[1152,384]{1,0:T(8,128)(2,1)}), bf16[1152,3072]{1,0:T(8,128)(2,1)}) %all-gather.4.cloned.1.call-update) | async-done | bytes 7077904 | tf_op jit(solution)/shard_map/all_gather | solution.py:105
  270.8 17.0 %convolution_add_fusion = f32[1152,1536]{1,0:T(8,128)} fusion(bf16[1152,3072]{1,0:T(8,128)(2,1)} %all-gather.4.cloned.1.call-done, bf16[3072,1536]{1,0:T(8,128)(2,1)} %all-gather.6.cloned.1.call-done, f32[1536]{0:T(1024)S(1)} %copy-done.97), kind=kOutput, calls=%fused_computation.7 | convolution fusion | flops 10873405440 | bytes 23599104 | tf_op jit(solution)/shard_map/dot_general | solution.py:104
  287.8 151.4 %all-gather.8.cloned.1.call-done = bf16[1536,3072]{1,0:T(8,128)(2,1)} async-done(((bf16[1536,768]{1,0:T(8,128)(2,1)}), bf16[1536,3072]{1,0:T(8,128)(2,1)}) %all-gather.8.cloned.1.call-update) | async-done | bytes 9437200 | tf_op jit(solution)/shard_map/all_gather | solution.py:90
  439.2 31.1 %fusion = bf16[3072,1152]{0,1:T(8,128)(2,1)} fusion(bf16[1536,3072]{1,0:T(8,128)(2,1)} %all-gather.8.cloned.1.call-done, f32[1152,1536]{1,0:T(8,128)} %convolution_add_fusion), kind=kOutput, calls=%fused_computation.5 | convolution fusion | flops 10990190592 | bytes 23592960 | tf_op jit(solution)/shard_map/dot_general | solution.py:111
  470.2 9.6 %copy.26 = bf16[3072,1152]{1,0:T(8,128)(2,1)} copy(bf16[3072,1152]{0,1:T(8,128)(2,1)} %fusion) | data formatting | bytes 14155776
  480.0 63.7 %reduce-scatter.7.cloned.1.call-done = bf16[384,1152]{1,0:T(8,128)(2,1)} async-done(((bf16[3072,1152]{1,0:T(8,128)(2,1)}), bf16[384,1152]{1,0:T(8,128)(2,1)}) %reduce-scatter.7.cloned.1.call-update) | async-done | bytes 884752
  548.7 18.3 %collective-permute-done = bf16[1152,384]{1,0:T(8,128)(2,1)S(1)} collective-permute-done((bf16[1152,384]{1,0:T(8,128)(2,1)S(1)}, bf16[1152,384]{1,0:T(8,128)(2,1)S(1)}, u32[]{:S(2)}, u32[]{:S(2)}) %collective-permute-start) | collective-permute-done | bytes 884768 | tf_op jit(solution)/shard_map/ppermute | solution.py:20
  569.9 15.0 %collective-permute-done.2 = bf16[1152,384]{1,0:T(8,128)(2,1)S(1)} collective-permute-done((bf16[1152,384]{1,0:T(8,128)(2,1)S(1)}, bf16[1152,384]{1,0:T(8,128)(2,1)S(1)}, u32[]{:S(2)}, u32[]{:S(2)}) %collective-permute-start.2) | collective-permute-done | bytes 884768 | tf_op jit(solution)/shard_map/ppermute | solution.py:20
  584.9 4.9 collective-permute-start.4
  598.5 14.0 %collective-permute-start.6 = (bf16[1152,384]{1,0:T(8,128)(2,1)S(1)}, bf16[1152,384]{1,0:T(8,128)(2,1)S(1)}, u32[]{:S(2)}, u32[]{:S(2)}) collective-permute-start(bf16[1152,384]{1,0:T(8,128)(2,1)S(1)} %collective-permute-done.4), channel_id=1, source_target_pairs={{0,1},{1,2},{2,3},{3,4},{4,5},{5,6},{6,7},{7,0},{8,9},{9,10},{10,1... | collective-permute-start | bytes 2654216 | tf_op jit(solution)/shard_map/ppermute | solution.py:20
  617.9 16.6 %fusion.2.clone.4 = bf16[1152,1536]{1,0:T(8,128)(2,1)S(1)} fusion(bf16[1152,3072]{1,0:T(8,128)(2,1)S(1)} %constant_dynamic-update-slice_fusion, bf16[1536,3072]{1,0:T(8,128)(2,1)} %all-gather.8.cloned.1.call-done, f32[1152,1536]{1,0:T(8,128)} %convolution_add_fusion), kind=kOutput, calls=%fused_computation.8.clone.clone.clone.1 | convolution fusion | flops 10889330688 | bytes 27131904 | tf_op jit(solution)/shard_map/dot_general | solution.py:126
  634.5 15.6 %fusion.1 = bf16[3072,1152]{0,1:T(8,128)(2,1)} fusion(bf16[3072,1536]{1,0:T(8,128)(2,1)} %all-gather.6.cloned.1.call-done, bf16[1152,1536]{1,0:T(8,128)(2,1)S(1)} %fusion.2.clone.4), kind=kOutput, calls=%fused_computation.6 | convolution fusion | flops 10875174912 | bytes 20054016 | tf_op jit(solution)/shard_map/dot_general | solution.py:135
  650.1 10.1 %copy.28 = bf16[3072,1152]{1,0:T(8,128)(2,1)} copy(bf16[3072,1152]{0,1:T(8,128)(2,1)} %fusion.1) | data formatting | bytes 14155776
  660.3 75.5 %reduce-scatter.9.cloned.1.call-done = bf16[384,1152]{1,0:T(8,128)(2,1)} async-done(((bf16[3072,1152]{1,0:T(8,128)(2,1)}), bf16[384,1152]{1,0:T(8,128)(2,1)}) %reduce-scatter.9.cloned.1.call-update) | async-done | bytes 884752
  738.7 21.2 %all-reduce.2 = (f32[1152]{0:T(1024)S(1)}, f32[1152]{0:T(1024)S(1)}) all-reduce(f32[1152]{0:T(1024)S(1)} %fusion.172, f32[1152]{0:T(1024)S(1)} %fusion.174), channel_id=1, replica_groups=mesh['row'=4,'col'=8] {'col'}, use_global_device_ids=true, to_apply=%region_9.10 | all-reduce | flops 2304 | bytes 18432 | tf_op jit(solution)/shard_map/psum | solution.py:55
  772.6 22.0 %all-to-all-done.2 = bf16[4,2,55296]{2,1,0:T(2,128)(2,1)S(1)} async-done(((bf16[4,2,55296]{2,1,0:T(2,128)(2,1)}), bf16[4,2,55296]{2,1,0:T(2,128)(2,1)S(1)}, u32[]{:S(2)}, u32[]{:S(2)}) %all-to-all-start.2) | async-done | bytes 884768 | tf_op jit(solution)/shard_map/all_to_all | solution.py:77
  800.5 19.4 %fusion.60 = bf16[96,48,96]{2,1,0:T(8,128)(2,1)S(1)} fusion(f32[102,54,96]{2,1,0:T(8,128)S(1)} %pad_convert_fusion, f32[96]{0:T(128)} %get-tuple-element.56, f32[96]{0:T(128)S(1)} %get-tuple-element.9, f32[96]{0:T(128)S(1)} %get-tuple-element.10, f32[96]{0:T(128)S(1)} %get-tuple-element.11, f32[96]{0:T(128)S(1)} %copy-done.17, f32[96]{0:T(128)S(1)} %copy-done.18, ...), kind=kLoop, calls=%fused_computation.74 | loop fusion | flops 46006272 | bytes 87608256 | tf_op jit(solution)/shard_map/convert_element_type | solution.py:83
  819.9 31.0 %all_to_all.72 = bf16[96,48,96]{2,1,0:T(8,128)(2,1)S(1)} all-to-all(bf16[96,48,96]{2,1,0:T(8,128)(2,1)S(1)} %fusion.60), channel_id=1, replica_groups=mesh['row'=4,'col'=8] {'row'}, dimensions={0} | all-to-all | bytes 1769472 | tf_op jit(solution)/shard_map/all_to_all | solution.py:84
  (265 shorter events, 72.5 us)
Async XLA Ops:
  7.2 211.9 %all-gather.6.cloned.1.call-start = ((), (), s32[]{:S(2)}) async-start(), calls=%async_computation.7 | async-start | bytes 11796480 | tf_op jit(solution)/shard_map/all_gather | solution.py:89
  14.4 55.7 %all-to-all-start = ((bf16[4,2,55296]{2,1,0:T(2,128)(2,1)}), bf16[4,2,55296]{2,1,0:T(2,128)(2,1)S(1)}, u32[]{:S(2)}, u32[]{:S(2)}) async-start(bf16[4,2,55296]{2,1,0:T(2,128)(2,1)} %reshape.134), calls=%async_computation | async-start | bytes 1769472 | tf_op jit(solution)/shard_map/all_to_all | solution.py:77
  96.1 59.8 %all-to-all-start.1 = ((bf16[96,48,96]{2,1,0:T(8,128)(2,1)}), bf16[96,48,96]{2,1,0:T(8,128)(2,1)S(1)}, u32[]{:S(2)}, u32[]{:S(2)}) async-start(bf16[96,48,96]{2,1,0:T(8,128)(2,1)} %fusion.115), calls=%async_computation.1 | async-start | bytes 2359296 | tf_op jit(solution)/shard_map/all_to_all | solution.py:84
  99.6 171.2 %all-gather.4.cloned.1.call-start = ((), (), s32[]{:S(2)}) async-start(), calls=%async_computation.6 | async-start | bytes 7962624 | tf_op jit(solution)/shard_map/all_gather | solution.py:105
  101.2 78.4 %copy-start.13 = (f32[384]{0:T(512)}, f32[384]{0:T(512)S(1)}, u32[]{:S(2)}) copy-start(f32[384]{0:T(512)S(1)} %dynamic_slice.13) | copy-start | bytes 4612
  180.2 90.6 %copy-start.97 = (f32[1536]{0:T(1024)S(1)}, f32[1536]{0:T(1024)}, u32[]{:S(2)}) copy-start(f32[1536]{0:T(1024)} %param.16) | copy-start | bytes 18436
  181.5 257.6 %all-gather.8.cloned.1.call-start = ((), (), s32[]{:S(2)}) async-start(), calls=%async_computation.8 | async-start | bytes 11796480 | tf_op jit(solution)/shard_map/all_gather | solution.py:90
  182.3 361.4 %reduce-scatter.7.cloned.1.call-start = ((), (), s32[]{:S(2)}) async-start(), calls=%async_computation.9 | async-start | bytes 7962624
  479.9 65.7 %copy-start.3 = (bf16[24,48,384]{2,1,0:T(8,128)(2,1)S(1)}, bf16[24,48,384]{2,1,0:T(8,128)(2,1)}, u32[]{:S(2)}) copy-start(bf16[24,48,384]{2,1,0:T(8,128)(2,1)} %param.10) | copy-start | bytes 2654212
  479.9 65.7 %copy-start.4 = (bf16[24,48,384]{2,1,0:T(8,128)(2,1)S(1)}, bf16[24,48,384]{2,1,0:T(8,128)(2,1)}, u32[]{:S(2)}) copy-start(bf16[24,48,384]{2,1,0:T(8,128)(2,1)} %param.11) | copy-start | bytes 2654212
  479.9 65.7 %copy-start.15 = (f32[384]{0:T(512)S(1)}, f32[384]{0:T(512)}, u32[]{:S(2)}) copy-start(f32[384]{0:T(512)} %param.19) | copy-start | bytes 4612
  479.9 255.9 %reduce-scatter.9.cloned.1.call-start = ((), (), s32[]{:S(2)}) async-start(), calls=%async_computation.10 | async-start | bytes 7962624
  547.0 20.0 %collective-permute-start = (bf16[1152,384]{1,0:T(8,128)(2,1)S(1)}, bf16[1152,384]{1,0:T(8,128)(2,1)S(1)}, u32[]{:S(2)}, u32[]{:S(2)}) collective-permute-start(bf16[1152,384]{1,0:T(8,128)(2,1)S(1)} %bitcast.271), channel_id=1, source_target_pairs={{0,1},{1,2},{2,3},{3,4},{4,5},{5,6},{6,7},{7,0},{8,9},{9,10},{10,1... | collective-permute-start | bytes 2654216 | tf_op jit(solution)/shard_map/ppermute | solution.py:20
  547.0 20.9 %collective-permute-start.1 = (bf16[1152,384]{1,0:T(8,128)(2,1)S(1)}, bf16[1152,384]{1,0:T(8,128)(2,1)}, u32[]{:S(2)}, u32[]{:S(2)}) collective-permute-start(bf16[1152,384]{1,0:T(8,128)(2,1)S(1)} %bitcast.272), channel_id=1, source_target_pairs={{0,7},{1,0},{2,1},{3,2},{4,3},{5,4},{6,5},{7,6},{8,15},{9,8},{10,9... | collective-permute-start | bytes 2654216 | tf_op jit(solution)/shard_map/ppermute | solution.py:23
  567.0 17.9 %collective-permute-start.2 = (bf16[1152,384]{1,0:T(8,128)(2,1)S(1)}, bf16[1152,384]{1,0:T(8,128)(2,1)S(1)}, u32[]{:S(2)}, u32[]{:S(2)}) collective-permute-start(bf16[1152,384]{1,0:T(8,128)(2,1)S(1)} %collective-permute-done), channel_id=1, source_target_pairs={{0,1},{1,2},{2,3},{3,4},{4,5},{5,6},{6,7},{7,0},{8,9},{9,10},{10,1... | collective-permute-start | bytes 2654216 | tf_op jit(solution)/shard_map/ppermute | solution.py:20
  567.9 24.2 %collective-permute-start.3 = (bf16[1152,384]{1,0:T(8,128)(2,1)}, bf16[1152,384]{1,0:T(8,128)(2,1)S(1)}, u32[]{:S(2)}, u32[]{:S(2)}) collective-permute-start(bf16[1152,384]{1,0:T(8,128)(2,1)} %collective-permute-done.1), channel_id=1, source_target_pairs={{0,7},{1,0},{2,1},{3,2},{4,3},{5,4},{6,5},{7,6},{8,15},{9,8},{10,9... | collective-permute-start | bytes 2654216 | tf_op jit(solution)/shard_map/ppermute | solution.py:23
  584.9 13.6 %collective-permute-start.4 = (bf16[1152,384]{1,0:T(8,128)(2,1)S(1)}, bf16[1152,384]{1,0:T(8,128)(2,1)S(1)}, u32[]{:S(2)}, u32[]{:S(2)}) collective-permute-start(bf16[1152,384]{1,0:T(8,128)(2,1)S(1)} %collective-permute-done.2), channel_id=1, source_target_pairs={{0,1},{1,2},{2,3},{3,4},{4,5},{5,6},{6,7},{7,0},{8,9},{9,10},{10,1... | collective-permute-start | bytes 2654216 | tf_op jit(solution)/shard_map/ppermute | solution.py:20
  592.1 21.1 %collective-permute-start.5 = (bf16[1152,384]{1,0:T(8,128)(2,1)S(1)}, bf16[1152,384]{1,0:T(8,128)(2,1)S(1)}, u32[]{:S(2)}, u32[]{:S(2)}) collective-permute-start(bf16[1152,384]{1,0:T(8,128)(2,1)S(1)} %collective-permute-done.3), channel_id=1, source_target_pairs={{0,7},{1,0},{2,1},{3,2},{4,3},{5,4},{6,5},{7,6},{8,15},{9,8},{10,9... | collective-permute-start | bytes 2654216 | tf_op jit(solution)/shard_map/ppermute | solution.py:23
  598.5 19.2 %collective-permute-start.6 = (bf16[1152,384]{1,0:T(8,128)(2,1)S(1)}, bf16[1152,384]{1,0:T(8,128)(2,1)S(1)}, u32[]{:S(2)}, u32[]{:S(2)}) collective-permute-start(bf16[1152,384]{1,0:T(8,128)(2,1)S(1)} %collective-permute-done.4), channel_id=1, source_target_pairs={{0,1},{1,2},{2,3},{3,4},{4,5},{5,6},{6,7},{7,0},{8,9},{9,10},{10,1... | collective-permute-start | bytes 2654216 | tf_op jit(solution)/shard_map/ppermute | solution.py:20
  660.3 77.3 %copy-start.10 = (f32[1152]{0:T(1024)S(1)}, f32[1152]{0:T(1024)}, u32[]{:S(2)}) copy-start(f32[1152]{0:T(1024)} %copy-done.9) | copy-start | bytes 13828
  660.3 77.4 %copy-start.12 = (f32[1152]{0:T(1024)S(1)}, f32[1152]{0:T(1024)}, u32[]{:S(2)}) copy-start(f32[1152]{0:T(1024)} %copy-done.11) | copy-start | bytes 13828
  660.3 77.4 %copy-start.14 = (f32[384]{0:T(512)S(1)}, f32[384]{0:T(512)}, u32[]{:S(2)}) copy-start(f32[384]{0:T(512)} %copy-done.13) | copy-start | bytes 4612
  660.3 77.3 %copy-start.1 = (bf16[24,48,384]{2,1,0:T(8,128)(2,1)S(1)}, bf16[24,48,384]{2,1,0:T(8,128)(2,1)}, u32[]{:S(2)}) copy-start(bf16[24,48,384]{2,1,0:T(8,128)(2,1)} %copy-done) | copy-start | bytes 2654212
  766.9 27.7 %all-to-all-start.2 = ((bf16[4,2,55296]{2,1,0:T(2,128)(2,1)}), bf16[4,2,55296]{2,1,0:T(2,128)(2,1)S(1)}, u32[]{:S(2)}, u32[]{:S(2)}) async-start(bf16[4,2,55296]{2,1,0:T(2,128)(2,1)} %reshape.136), calls=%async_computation.2 | async-start | bytes 1769472 | tf_op jit(solution)/shard_map/all_to_all | solution.py:77
  (89 other events, 186.7 us)
Sparse Core Ops, SparseCore 0:
  9.6 209.4 all-gather.5
  221.5 49.2 all-gather.3
  272.4 166.7 all-gather.7
  480.0 63.5 reduce-scatter.6
  660.4 75.3 reduce-scatter.8
